TPU v7x, 32 devices: a whole 2x2x4 slice. The times are simulated.
32 devices in a mesh: members: 2 (over y), cards: 4 (over z), sub: 2 (over x), rep: 2 (over core).
Axes of the slice: x: 2, y: 2, z: 4, core: 2. Of those that a mesh axis runs over, the one named last changes fastest.
Arguments:
- spectra: float32 [36, 32, 2, 8192], P('rep', None, 'sub', ('members', 'cards')), parts along dimension 3, may hold values from 0.02 to 0.6
- deal_slot: int32 [2, 8192], P('sub', 'members'), parts along dimension 1, may hold values from 0 to 4095, each once within a row
- sea_mask: int32 [32, 512], P('sub', 'members'), parts along dimension 1, may hold values 0 or 1
- ice_class: int32 [2, 8192], P('sub', ('members', 'cards')), parts along dimension 1, may hold values from 0 to 3
- brine: float32 [2, 8192], P('sub', ('members', 'cards')), parts along dimension 1, may hold values from 0.02 to 0.3
- wind_rate: float32 [2, 8192], P('sub', ('members', 'cards')), parts along dimension 1, may hold values from 0 to 0.6
- wind_dir: float32 [2, 8192], P('sub', ('members', 'cards')), parts along dimension 1, may hold values from -3.140625 to 3.140625
- ice_table: float32 [4, 32], replicated, may hold values from 0.05 to 1.5
Outputs:
- spectra_out: float32 [36, 32, 2, 8192], P('rep', None, 'sub', ('members', 'cards')), parts along dimension 3
There are 2 independent parts, one for each index of `members`. A program takes and returns all parts, laid end to end along the dimension named above; an argument that names none is the same for every part. Nothing has to cross between parts.
Inputs may be any that keep to these rules, and one draw needn't show every extreme that they name: `deal_slot`: each row is a permutation of the slots of its row block.
All inputs are finite; a program needn't handle non-finite values. No bound on the sum of `sea_mask` on one device may be relied on, other than what follows from the above.
Results may differ from a plain program's by a relative error of at most 0.000098.
Values sent between devices are 32-bit elements; how exact they have to be, the bound alone decides.
A program may use at most 64 MiB of HBM per device.

v0:
```python
import jax
import jax.numpy as jnp
from jax import lax
from jax.sharding import PartitionSpec as P

NSTEP = 2


F0 = 0.035
GROWTH = 1.1
CNL = 0.25
COURANT = 0.6


def extended(block, sides, width, periodic):
    for axis, dim in sides:
        count = lax.axis_size(axis)
        forward = [(i, i + 1) for i in range(count - 1)]
        if periodic:
            forward.append((count - 1, 0))
        backward = [(target, source) for source, target in forward]
        low = lax.ppermute(
            lax.slice_in_dim(block, block.shape[dim] - width, None, axis=dim), axis, forward
        )
        high = lax.ppermute(lax.slice_in_dim(block, 0, width, axis=dim), axis, backward)
        block = jnp.concatenate([low, block, high], axis=dim)
    return block


def freq_up(x):
    return jnp.concatenate([x[:, 1:], jnp.zeros_like(x[:, :1])], axis=1)


def freq_down(x):
    return jnp.concatenate([jnp.zeros_like(x[:, :1]), x[:, :-1]], axis=1)


def dir_pair(energy):
    framed = extended(energy, (("rep", 0),), 1, True)
    return (framed[2:], framed[:-2])


def nonlinear(energy, pone, mone, ptwo, mtwo):
    return CNL * (
        energy * energy * (pone + mone + ptwo + mtwo) - 2.0 * energy * (pone * mone + ptwo * mtwo)
    )


def shards(spectra, deal_slot, sea_mask, ice_class, brine, wind_rate, wind_dir, ice_table):
    dir_count, freq_count, _, point_count = spectra.shape
    card_count = lax.axis_size("cards")
    rep_count = lax.axis_size("rep")
    rep_index = lax.axis_index("rep")
    all_dirs_count = dir_count * rep_count
    theta_all = 2.0 * jnp.pi * jnp.arange(all_dirs_count, dtype=jnp.float32) / all_dirs_count
    theta = lax.dynamic_slice_in_dim(theta_all, rep_index * dir_count, dir_count, 0)
    freq = F0 * GROWTH ** jnp.arange(freq_count, dtype=jnp.float32)
    speed = COURANT * (freq[0] / freq)
    class_count = ice_table.shape[0]
    slot_of = deal_slot[0]
    block_cells = slot_of.shape[0]
    cell_of = (
        jnp.zeros((block_cells,), jnp.int32)
        .at[slot_of]
        .set(jnp.arange(block_cells, dtype=jnp.int32))
    )
    rows_here, columns = sea_mask.shape
    maskf = sea_mask.astype(jnp.float32)[None]
    energy = spectra[:, :, 0, :]
    velocity = jnp.stack(
        [jnp.cos(theta)[:, None] * speed[None, :], jnp.sin(theta)[:, None] * speed[None, :]],
        axis=-1,
    )
    per_card = dir_count * freq_count // card_count
    velocity = velocity.reshape(per_card, card_count, 2)
    beta = (
        wind_rate[0][None, None, :]
        * jnp.maximum(jnp.cos(theta[:, None, None] - wind_dir[0][None, None, :]), 0.0)
        * (freq / freq[-1])[None, :, None]
    )
    onehot = (ice_class[0][None, :] == jnp.arange(class_count, dtype=jnp.int32)[:, None]).astype(
        jnp.float32
    )
    rate = jnp.dot(
        ice_table.T, onehot, precision=lax.Precision.HIGHEST, preferred_element_type=jnp.float32
    )
    rate = rate * jnp.sqrt(brine[0] / 0.1)[None, :]
    growth = jnp.exp(beta - rate[None])
    for step in range(NSTEP):
        plus_d, minus_d = dir_pair(energy)
        nonlin = nonlinear(
            energy, freq_up(plus_d), freq_down(minus_d), freq_up(minus_d), freq_down(plus_d)
        )
        energy = energy * growth + nonlin
        moving = energy.reshape(per_card, card_count, point_count)
        arrived, speeds = (
            lax.all_to_all(moving, "cards", split_axis=1, concat_axis=2, tiled=True),
            lax.all_to_all(velocity, "cards", split_axis=1, concat_axis=2, tiled=True),
        )
        items = arrived.shape[0]
        grid = jnp.take(arrived[:, 0, :], slot_of, axis=1).reshape(items, rows_here, columns)
        nux = speeds[:, 0, 0][:, None, None]
        nuy = speeds[:, 0, 1][:, None, None]
        framed = extended(grid, (("sub", 1),), 1, False)
        below = framed[:, :-2, :]
        above = framed[:, 2:, :]
        left = jnp.pad(grid, ((0, 0), (0, 0), (1, 0)))[..., :-1]
        right = jnp.pad(grid, ((0, 0), (0, 0), (0, 1)))[..., 1:]
        moved = (
            grid
            - jnp.maximum(nux, 0.0) * (grid - left)
            - jnp.minimum(nux, 0.0) * (right - grid)
            - jnp.maximum(nuy, 0.0) * (grid - below)
            - jnp.minimum(nuy, 0.0) * (above - grid)
        )
        moved = moved * maskf
        done = jnp.take(moved.reshape(items, block_cells), cell_of, axis=1)[:, None, :]
        back = lax.all_to_all(done, "cards", split_axis=2, concat_axis=1, tiled=True)
        energy = back.reshape(dir_count, freq_count, point_count)
    return energy[:, :, None, :]


def solution(mesh):
    placed = (
        P("rep", None, "sub", ("members", "cards")),
        P("sub", "members"),
        P("sub", "members"),
        P("sub", ("members", "cards")),
        P("sub", ("members", "cards")),
        P("sub", ("members", "cards")),
        P("sub", ("members", "cards")),
        P(),
    )
    return jax.shard_map(
        shards,
        mesh=mesh,
        in_specs=placed,
        out_specs=P("rep", None, "sub", ("members", "cards")),
        check_vma=False,
    )
```

profile of v0, /device:TPU:0, one launch (start us, length us, event | category | flops | bytes accessed | tf_op | source)
XLA Modules:
  0.0 541.0 jit_solution(14812608059823682782)
XLA Ops:
  2.8 6.3 %all-to-all-start.1 = ((f32[144,4,2]{0,2,1:T(2,128)}), f32[144,4,2]{0,2,1:T(2,128)S(1)}, u32[]{:S(2)}, u32[]{:S(2)}) async-start(f32[144,4,2]{0,2,1:T(2,128)} %copy.43), calls=%async_computation.1 | async-start | bytes 16384 | tf_op jit(solution)/shard_map/all_to_all | solution.py:98
  21.4 4.5 copy.41
  25.8 5.2 all-to-all-start
  31.1 15.5 %scatter_custom_fusion = s32[4096]{0:T(1024)S(1)} fusion(s32[4096]{0:T(1024)S(1)} %bitcast.72, s32[4096]{0:T(1024)S(1)} %iota.25, s32[]{:T(128)} %constant.6.clone.1), kind=kCustom, calls=%fused_computation.77 | custom fusion | bytes 16388 | tf_op jit(solution)/shard_map/scatter | solution.py:65
  46.7 38.3 %all-to-all-done = f32[144,4,1024]{2,0,1:T(8,128)S(1)} async-done(((f32[144,4,1024]{2,0,1:T(8,128)}), f32[144,4,1024]{2,0,1:T(8,128)S(1)}, u32[]{:S(2)}, u32[]{:S(2)}) %all-to-all-start) | async-done | bytes 2359328 | tf_op jit(solution)/shard_map/all_to_all | solution.py:97
  88.5 18.3 %gather_fusion = f32[4096,144]{1,0:T(8,128)} fusion(f32[144,4096]{0,1:T(8,128)} %bitcast.60, s32[4096]{0:T(1024)S(1)} %fusion.29), kind=kCustom, calls=%fused_computation.clone | custom fusion | bytes 4734976 | tf_op jit(solution)/shard_map/jit(_take)/gather | solution.py:101
  106.8 4.1 broadcast_select_fusion.1
  119.1 4.1 collective-permute-done.3
  123.2 4.3 fusion.6
  127.5 18.3 %gather_fusion.1 = f32[4096,144]{1,0:T(8,128)} fusion(f32[144,4096]{0,1:T(8,128)} %bitcast.58, s32[4096]{0:T(1024)S(1)} %fusion.30), kind=kCustom, calls=%fused_computation.1.clone | custom fusion | bytes 4734976 | tf_op jit(solution)/shard_map/jit(_take)/gather | solution.py:117
  150.0 17.0 %copy.44 = f32[144,1,4096]{0,1,2:T(1,128)S(1)} copy(f32[144,1,4096]{0,2,1:T(8,128)S(1)} %select_bitcast_fusion.1) | data formatting | bytes 4718592 | tf_op jit(solution)/shard_map/broadcast_in_dim | solution.py:117
  166.9 94.0 %all_to_all.23 = f32[144,1,4096]{0,1,2:T(1,128)S(1)} all-to-all(f32[144,1,4096]{0,1,2:T(1,128)S(1)} %copy.44), channel_id=1, replica_groups=mesh['members'=2,'cards'=4,'sub'=2,'rep'=2] {'cards'}, dimensions={2} | all-to-all | bytes 4718592 | tf_op jit(solution)/shard_map/all_to_all | solution.py:118
  261.0 6.5 %fusion.36 = (f32[8,1,4096]{0,1,2:T(1,128)S(1)}, f32[8,1,4096]{0,1,2:T(1,128)}) fusion(f32[144,1,4096]{0,1,2:T(1,128)S(1)} %all_to_all.23), kind=kLoop, calls=%fused_computation.91 | loop fusion | bytes 524288 | tf_op jit(solution)/shard_map/slice | solution.py:23
  269.5 9.8 %copy.45 = f32[144,1,4096]{2,0,1:T(8,128)} copy(f32[144,1,4096]{0,1,2:T(1,128)} %copy-done.2) | data formatting | bytes 4718592 | tf_op jit(solution)/shard_map/all_to_all | solution.py:118
  281.9 4.4 copy.46
  296.1 56.8 %all_to_all.24 = f32[144,4,1024]{2,0,1:T(8,128)S(1)} all-to-all(f32[144,4,1024]{2,0,1:T(8,128)S(1)} %copy.48), channel_id=1, replica_groups=mesh['members'=2,'cards'=4,'sub'=2,'rep'=2] {'cards'}, dimensions={1} | all-to-all | bytes 4718592 | tf_op jit(solution)/shard_map/all_to_all | solution.py:97
  356.3 18.3 %gather_fusion.2 = f32[4096,144]{1,0:T(8,128)} fusion(f32[144,4096]{0,1:T(8,128)} %bitcast.59, s32[4096]{0:T(1024)S(1)} %fusion.29), kind=kCustom, calls=%fused_computation.2.clone | custom fusion | bytes 4734976 | tf_op jit(solution)/shard_map/jit(_take)/gather | solution.py:101
  374.6 4.1 broadcast_select_fusion
  385.2 4.1 collective-permute-done.7
  389.3 4.3 fusion.15
  393.6 18.3 %gather_fusion.3 = f32[4096,144]{1,0:T(8,128)} fusion(f32[144,4096]{0,1:T(8,128)} %bitcast.57, s32[4096]{0:T(1024)S(1)} %fusion.30), kind=kCustom, calls=%fused_computation.3.clone | custom fusion | bytes 4734976 | tf_op jit(solution)/shard_map/jit(_take)/gather | solution.py:117
  416.0 17.0 %copy.50 = f32[144,1,4096]{0,1,2:T(1,128)S(1)} copy(f32[144,1,4096]{0,2,1:T(8,128)S(1)} %select_bitcast_fusion) | data formatting | bytes 4718592 | tf_op jit(solution)/shard_map/broadcast_in_dim | solution.py:117
  433.0 95.1 %all_to_all.25 = f32[144,1,4096]{0,1,2:T(1,128)} all-to-all(f32[144,1,4096]{0,1,2:T(1,128)S(1)} %copy.50), channel_id=1, replica_groups=mesh['members'=2,'cards'=4,'sub'=2,'rep'=2] {'cards'}, dimensions={2} | all-to-all | bytes 4718592 | tf_op jit(solution)/shard_map/all_to_all | solution.py:118
  528.1 9.1 %copy.51 = f32[144,1,4096]{2,0,1:T(8,128)S(1)} copy(f32[144,1,4096]{0,1,2:T(1,128)} %all_to_all.25) | data formatting | bytes 4718592 | tf_op jit(solution)/shard_map/all_to_all | solution.py:118
  (79 shorter events, 62.8 us)
Async XLA Ops:
  0.0 11.5 %copy-start = (f32[4,32]{1,0:T(4,128)S(1)}, f32[4,32]{1,0:T(4,128)}, u32[]{:S(2)}) copy-start(f32[4,32]{1,0:T(4,128)} %param.17) | copy-start | bytes 1540
  2.8 23.1 %all-to-all-start.1 = ((f32[144,4,2]{0,2,1:T(2,128)}), f32[144,4,2]{0,2,1:T(2,128)S(1)}, u32[]{:S(2)}, u32[]{:S(2)}) async-start(f32[144,4,2]{0,2,1:T(2,128)} %copy.43), calls=%async_computation.1 | async-start | bytes 16384 | tf_op jit(solution)/shard_map/all_to_all | solution.py:98
  10.1 6.3 %collective-permute-start = (f32[1,32,1024]{2,1,0:T(8,128)S(1)}, f32[1,32,1024]{2,1,0:T(8,128)S(1)}, u32[]{:S(2)}, u32[]{:S(2)}) collective-permute-start(f32[1,32,1024]{2,1,0:T(8,128)S(1)} %bitcast.69), channel_id=1, source_target_pairs={{1,0},{0,1},{3,2},{2,3},{5,4},{4,5},{7,6},{6,7},{9,8},{8,9},{11,10... | collective-permute-start | bytes 393224 | tf_op jit(solution)/shard_map/ppermute | solution.py:25
  10.2 6.2 %collective-permute-start.1 = (f32[1,32,1024]{2,1,0:T(8,128)S(1)}, f32[1,32,1024]{2,1,0:T(8,128)S(1)}, u32[]{:S(2)}, u32[]{:S(2)}) collective-permute-start(f32[1,32,1024]{2,1,0:T(8,128)S(1)} %bitcast.70), channel_id=1, source_target_pairs={{0,1},{1,0},{2,3},{3,2},{4,5},{5,4},{6,7},{7,6},{8,9},{9,8},{10,11... | collective-permute-start | bytes 393224 | tf_op jit(solution)/shard_map/ppermute | solution.py:22
  25.8 5.2 copy-start.4
  25.8 5.2 copy-start.3
  25.8 59.2 %all-to-all-start = ((f32[144,4,1024]{2,0,1:T(8,128)}), f32[144,4,1024]{2,0,1:T(8,128)S(1)}, u32[]{:S(2)}, u32[]{:S(2)}) async-start(f32[144,4,1024]{2,0,1:T(8,128)} %copy.41), calls=%async_computation | async-start | bytes 4718592 | tf_op jit(solution)/shard_map/all_to_all | solution.py:97
  110.9 8.2 %collective-permute-start.2 = (f32[144,1,256]{0,2,1:T(8,128)S(1)}, f32[144,1,256]{0,2,1:T(8,128)S(1)}, u32[]{:S(2)}, u32[]{:S(2)}) collective-permute-start(f32[144,1,256]{0,2,1:T(8,128)S(1)} %get-tuple-element.12), channel_id=1, source_target_pairs={{0,2},{1,3},{4,6},{5,7},{8,10},{9,11},{12,14},{13,15},{16,18},{17,... | collective-permute-start | bytes 442376 | tf_op jit(solution)/shard_map/ppermute | solution.py:22
  114.3 8.9 %collective-permute-start.3 = (f32[144,1,256]{0,2,1:T(8,128)S(1)}, f32[144,1,256]{0,2,1:T(8,128)S(1)}, u32[]{:S(2)}, u32[]{:S(2)}) collective-permute-start(f32[144,1,256]{0,2,1:T(8,128)S(1)} %get-tuple-element.13), channel_id=1, source_target_pairs={{2,0},{3,1},{6,4},{7,5},{10,8},{11,9},{14,12},{15,13},{18,16},{19,... | collective-permute-start | bytes 442376 | tf_op jit(solution)/shard_map/ppermute | solution.py:25
  261.0 6.5 %copy-start.2 = (f32[144,1,4096]{0,1,2:T(1,128)}, f32[144,1,4096]{0,1,2:T(1,128)S(1)}, u32[]{:S(2)}) copy-start(f32[144,1,4096]{0,1,2:T(1,128)S(1)} %all_to_all.23) | copy-start | bytes 7077892
  269.4 17.4 %collective-permute-start.5 = (f32[1,32,1024]{2,1,0:T(8,128)S(1)}, f32[1,32,1024]{2,1,0:T(8,128)S(1)}, u32[]{:S(2)}, u32[]{:S(2)}) collective-permute-start(f32[1,32,1024]{2,1,0:T(8,128)S(1)} %slice.140), channel_id=1, source_target_pairs={{0,1},{1,0},{2,3},{3,2},{4,5},{5,4},{6,7},{7,6},{8,9},{9,8},{10,11... | collective-permute-start | bytes 393224 | tf_op jit(solution)/shard_map/ppermute | solution.py:22
  286.3 1.9 collective-permute-start.4
  378.7 6.4 %collective-permute-start.6 = (f32[144,1,256]{0,2,1:T(8,128)S(1)}, f32[144,1,256]{0,2,1:T(8,128)S(1)}, u32[]{:S(2)}, u32[]{:S(2)}) collective-permute-start(f32[144,1,256]{0,2,1:T(8,128)S(1)} %get-tuple-element.8), channel_id=1, source_target_pairs={{0,2},{1,3},{4,6},{5,7},{8,10},{9,11},{12,14},{13,15},{16,18},{17,... | collective-permute-start | bytes 442376 | tf_op jit(solution)/shard_map/ppermute | solution.py:22
  380.2 9.1 %collective-permute-start.7 = (f32[144,1,256]{0,2,1:T(8,128)S(1)}, f32[144,1,256]{0,2,1:T(8,128)S(1)}, u32[]{:S(2)}, u32[]{:S(2)}) collective-permute-start(f32[144,1,256]{0,2,1:T(8,128)S(1)} %get-tuple-element.9), channel_id=1, source_target_pairs={{2,0},{3,1},{6,4},{7,5},{10,8},{11,9},{14,12},{15,13},{18,16},{19,... | collective-permute-start | bytes 442376 | tf_op jit(solution)/shard_map/ppermute | solution.py:25
  528.1 12.9 %copy-start.1 = (f32[4,32]{1,0:T(4,128)S(1)}, f32[4,32]{1,0:T(4,128)}, u32[]{:S(2)}) copy-start(f32[4,32]{1,0:T(4,128)} %param.17) | copy-start | bytes 1540
where the time goes:
time: 543 us; the launch traced here: 541 us
  blocking collectives  246 us (45%)
  local copies, waits for them, and re-layouts  185 us (34%)
  waiting for transfers between devices  53.7 us (10%)
  other arithmetic  34.6 us (6%)
  starting transfers between devices  20.3 us (4%)
    all_to_all x2, blocking collectives, shards(): lax.all_to_all(done, 'cards', split_axis=2, concat_axis=1, tiled=True)  189 us
    all_to_all x1, blocking collectives, shards(): lax.all_to_all(moving, 'cards', split_axis=1, concat_axis=2, tiled=True)  56.8 us
    all_to_all x1, waiting for transfers between devices, shards(): lax.all_to_all(moving, 'cards', split_axis=1, concat_axis=2, tiled=True)  38.3 us
    gather x2, local copies, waits for them, and re-layouts, shards(): jnp.take(arrived[:, 0, :], slot_of, axis=1)  36.6 us
    gather x2, local copies, waits for them, and re-layouts, shards(): jnp.take(moved.reshape(items, block_cells), cell_of, axis=1)[:, None, :]  36.6 us
    broadcast_in_dim x2, local copies, waits for them, and re-layouts, shards(): jnp.take(moved.reshape(items, block_cells), cell_of, axis=1)[:, None, :]  33.9 us
    all_to_all x2, local copies, waits for them, and re-layouts, shards(): lax.all_to_all(done, 'cards', split_axis=2, concat_axis=1, tiled=True)  18.8 us
    scatter x1, local copies, waits for them, and re-layouts, shards(): cell_of = jnp.zeros((block_cells,), jnp.int32).at[slot_of].set(jnp.arange...  15.5 us
  transfers between devices with their start and end apart: 10, of which 5 were waited for; matrix products, arithmetic and copies ran while one was open for 9% of the time, Pallas kernels for 0%

commit v1 on v0

v1 whole, which is shorter than its diff:
```python
import jax
import jax.numpy as jnp
from jax import lax
from jax.sharding import PartitionSpec as P

NSTEP = 2


F0 = 0.035
GROWTH = 1.1
CNL = 0.25
COURANT = 0.6


def extended(block, sides, width, periodic):
    for axis, dim in sides:
        count = lax.axis_size(axis)
        forward = [(i, i + 1) for i in range(count - 1)]
        if periodic:
            forward.append((count - 1, 0))
        backward = [(target, source) for source, target in forward]
        low = lax.ppermute(
            lax.slice_in_dim(block, block.shape[dim] - width, None, axis=dim), axis, forward
        )
        high = lax.ppermute(lax.slice_in_dim(block, 0, width, axis=dim), axis, backward)
        block = jnp.concatenate([low, block, high], axis=dim)
    return block


def freq_up(x):
    return jnp.concatenate([x[:, 1:], jnp.zeros_like(x[:, :1])], axis=1)


def freq_down(x):
    return jnp.concatenate([jnp.zeros_like(x[:, :1]), x[:, :-1]], axis=1)


def dir_pair(energy):
    framed = extended(energy, (("rep", 0),), 1, True)
    return (framed[2:], framed[:-2])


def nonlinear(energy, pone, mone, ptwo, mtwo):
    return CNL * (
        energy * energy * (pone + mone + ptwo + mtwo) - 2.0 * energy * (pone * mone + ptwo * mtwo)
    )


def edges(block, axis, dim, width):
    count = lax.axis_size(axis)
    forward = [(i, i + 1) for i in range(count - 1)]
    backward = [(i + 1, i) for i in range(count - 1)]
    size = block.shape[dim]
    low = lax.ppermute(lax.slice_in_dim(block, size - width, None, axis=dim), axis, forward)
    high = lax.ppermute(lax.slice_in_dim(block, 0, width, axis=dim), axis, backward)
    return low, high


def propagate(grid, nux, nuy, maskf):
    framed = extended(grid, (("sub", 2),), 1, False)
    below = framed[:, :, :-2, :]
    above = framed[:, :, 2:, :]
    left = jnp.pad(grid, ((0, 0), (0, 0), (0, 0), (1, 0)))[..., :-1]
    right = jnp.pad(grid, ((0, 0), (0, 0), (0, 0), (0, 1)))[..., 1:]
    moved = (
        grid
        - jnp.maximum(nux, 0.0) * (grid - left)
        - jnp.minimum(nux, 0.0) * (right - grid)
        - jnp.maximum(nuy, 0.0) * (grid - below)
        - jnp.minimum(nuy, 0.0) * (above - grid)
    )
    return moved * maskf


def growth_of(theta, freq_ratio, table, classes, brine, wind_rate, wind_dir):
    beta = (
        wind_rate[None, None, :]
        * jnp.maximum(jnp.cos(theta[:, None, None] - wind_dir[None, None, :]), 0.0)
        * freq_ratio[None, :, None]
    )
    rate = jnp.zeros((table.shape[1], classes.shape[0]), jnp.float32)
    for k in range(table.shape[0]):
        rate = jnp.where(classes[None, :] == k, table[k][:, None], rate)
    rate = rate * jnp.sqrt(brine / 0.1)[None, :]
    return jnp.exp(beta - rate[None])


def shards(spectra, deal_slot, sea_mask, ice_class, brine, wind_rate, wind_dir, ice_table):
    dir_count, freq_count, _, point_count = spectra.shape
    card_count = lax.axis_size("cards")
    card = lax.axis_index("cards")
    rep_count = lax.axis_size("rep")
    rep_index = lax.axis_index("rep")
    own = freq_count // card_count
    all_dirs_count = dir_count * rep_count
    theta_all = 2.0 * jnp.pi * jnp.arange(all_dirs_count, dtype=jnp.float32) / all_dirs_count
    theta = lax.dynamic_slice_in_dim(theta_all, rep_index * dir_count, dir_count, 0)
    freq = F0 * GROWTH ** jnp.arange(freq_count, dtype=jnp.float32)
    speed = lax.dynamic_slice_in_dim(COURANT * (freq[0] / freq), card * own, own, 0)
    ratio = freq / freq[-1]
    slot_of = deal_slot[0]
    block_cells = slot_of.shape[0]
    cell_of = (
        jnp.zeros((block_cells,), jnp.int32)
        .at[slot_of]
        .set(jnp.arange(block_cells, dtype=jnp.int32))
    )
    rows_here, columns = sea_mask.shape
    maskf = sea_mask.astype(jnp.float32)[None, None]
    energy = spectra[:, :, 0, :]
    nux = (jnp.cos(theta)[:, None] * speed[None, :])[:, :, None, None]
    nuy = (jnp.sin(theta)[:, None] * speed[None, :])[:, :, None, None]

    growth = growth_of(
        theta, ratio, ice_table, ice_class[0], brine[0], wind_rate[0], wind_dir[0]
    )
    points = jnp.stack([ice_class[0].astype(jnp.float32), brine[0], wind_rate[0], wind_dir[0]])
    points = lax.all_gather(points, "cards", axis=1, tiled=True)
    points = jnp.take(points, slot_of, axis=1)
    growth_own = growth_of(
        theta,
        lax.dynamic_slice_in_dim(ratio, card * own, own, 0),
        lax.dynamic_slice_in_dim(ice_table, card * own, own, 1),
        points[0].astype(jnp.int32), points[1], points[2], points[3],
    )

    plus_d, minus_d = dir_pair(energy)
    nonlin = nonlinear(
        energy, freq_up(plus_d), freq_down(minus_d), freq_up(minus_d), freq_down(plus_d)
    )
    energy = energy * growth + nonlin
    energy = lax.all_to_all(energy, "cards", split_axis=1, concat_axis=2, tiled=True)
    grid = jnp.take(energy, slot_of, axis=2).reshape(dir_count, own, rows_here, columns)
    for step in range(NSTEP):
        if step > 0:
            flat = grid.reshape(dir_count, own, block_cells)
            low, high = edges(flat, "cards", 1, 1)
            tall = extended(jnp.concatenate([low, flat, high], axis=1), (("rep", 0),), 1, True)
            plus_d, minus_d = tall[2:], tall[:-2]
            nonlin = nonlinear(
                flat, plus_d[:, 2:], minus_d[:, :-2], minus_d[:, 2:], plus_d[:, :-2]
            )
            grid = (flat * growth_own + nonlin).reshape(dir_count, own, rows_here, columns)
        grid = propagate(grid, nux, nuy, maskf)
    done = jnp.take(grid.reshape(dir_count, own, block_cells), cell_of, axis=2)
    energy = lax.all_to_all(done, "cards", split_axis=2, concat_axis=1, tiled=True)
    return energy[:, :, None, :]


def solution(mesh):
    placed = (
        P("rep", None, "sub", ("members", "cards")),
        P("sub", "members"),
        P("sub", "members"),
        P("sub", ("members", "cards")),
        P("sub", ("members", "cards")),
        P("sub", ("members", "cards")),
        P("sub", ("members", "cards")),
        P(),
    )
    return jax.shard_map(
        shards,
        mesh=mesh,
        in_specs=placed,
        out_specs=P("rep", None, "sub", ("members", "cards")),
        check_vma=False,
    )
```

time: 543 us -> 496 us (0.913)
  blocking collectives: 246 us -> 158 us
  other arithmetic: 34.6 us -> 83.9 us
  waiting for transfers between devices: 53.7 us -> 16.9 us
  local copies, waits for them, and re-layouts: 185 us -> 208 us
    all_to_all x2 -> x1, blocking collectives: 189 us -> 56.8 us  [shards(): lax.all_to_all(done, 'cards', split_axis=2, concat_axis=1, tiled=True)]
    all_gather x0 -> x1, blocking collectives: none -> 101 us  [shards(): points = lax.all_gather(points, 'cards', axis=1, tiled=True)]
    all_to_all x1 -> x0, blocking collectives: 56.8 us -> none  [shards(): lax.all_to_all(moving, 'cards', split_axis=1, concat_axis=2, tiled=True)]
    unnamed x14 -> x69, local copies, waits for them, and re-layouts: 2.28 us -> 51 us
    all_to_all x2 -> x1, waiting for transfers between devices: 38.3 us -> 0.01 us  [shards(): lax.all_to_all(energy, 'cards', split_axis=1, concat_axis=2, tiled=True)]
    broadcast_in_dim x2 -> x3, local copies, waits for them, and re-layouts: 33.9 us -> 4.67 us  [the longest x1 3.83 us: shards(): return energy[:, :, None, :]]
    unnamed x0 -> x1, other arithmetic: none -> 17 us
    gather x4 -> x3, local copies, waits for them, and re-layouts: 73.3 us -> 89.4 us  [the longest x1 36.9 us: shards(): jnp.take(energy, slot_of, axis=2)]
  transfers between devices with their start and end apart: 10 -> 11, of which waited for: 5 -> 7; matrix products, arithmetic and copies ran while one was open for 9% -> 12% of each run, Pallas kernels for 0% -> 0%
where the time goes in v1:
time: 496 us; the launch traced here: 489 us
  local copies, waits for them, and re-layouts  208 us (42%)
  blocking collectives  158 us (32%)
  other arithmetic  83.9 us (17%)
  starting transfers between devices  21.7 us (4%)
  waiting for transfers between devices  16.9 us (3%)
    all_gather x1, blocking collectives, shards(): points = lax.all_gather(points, 'cards', axis=1, tiled=True)  101 us
    all_to_all x1, blocking collectives, shards(): lax.all_to_all(done, 'cards', split_axis=2, concat_axis=1, tiled=True)  56.8 us
    unnamed x69, local copies, waits for them, and re-layouts  51 us
    gather x1, local copies, waits for them, and re-layouts, shards(): jnp.take(energy, slot_of, axis=2)  36.9 us
    gather x1, local copies, waits for them, and re-layouts, shards(): done = jnp.take(grid.reshape(dir_count, own, block_cells), cell_of, axis=2)  36.8 us
    unnamed x1, other arithmetic  17 us
    select_n x1, other arithmetic, shards(): jnp.take(energy, slot_of, axis=2)  17 us
    scatter x1, local copies, waits for them, and re-layouts, shards(): cell_of = jnp.zeros((block_cells,), jnp.int32).at[slot_of].set(jnp.arange...  16.2 us
  transfers between devices with their start and end apart: 11, of which 7 were waited for; matrix products, arithmetic and copies ran while one was open for 12% of the time, Pallas kernels for 0%

profile of v1, /device:TPU:0, one launch (start us, length us, event | category | flops | bytes accessed | tf_op | source)
XLA Modules:
  0.0 489.5 jit_solution(15092838402147379941)
XLA Ops:
  11.8 6.2 %multiply_add_fusion = f32[18,32,1024]{2,0,1:T(8,128)} fusion(f32[18,32,1024]{2,0,1:T(8,128)S(1)} %bitcast.63, f32[1,32,1024]{2,0,1:T(1,128)S(1)} %collective-permute-done, f32[1,32,1024]{2,0,1:T(1,128)S(1)} %collective-permute-done.1, f32[18,31,1024]{2,0,1:T(8,128)S(1)} %get-tuple-element.28, f32[18,31,1024]{2,0,1:T(8,128)S(1)} %get-tuple-element.27, ...), kind=kLoop, calls=%fused_computation.28 | loop fusion | flops 14155776 | bytes 9756800 | tf_op jit(solution)/shard_map/add | solution.py:131
  18.0 6.4 %all-to-all-start = ((f32[18,32,1024]{2,0,1:T(8,128)}), f32[18,32,1024]{2,0,1:T(8,128)S(1)}, u32[]{:S(2)}, u32[]{:S(2)}) async-start(f32[18,32,1024]{2,0,1:T(8,128)} %multiply_add_fusion), calls=%async_computation | async-start | bytes 6291456 | tf_op jit(solution)/shard_map/all_to_all | solution.py:132
  26.3 101.4 %all_gather.3 = f32[4,4096]{0,1:T(8,128)} all-gather(f32[4,1024]{0,1:T(8,128)} %copy.47), channel_id=1, replica_groups=mesh['members'=2,'cards'=4,'sub'=2,'rep'=2] {'cards'}, dimensions={1}, use_global_device_ids=true | all-gather | bytes 81920 | tf_op jit(solution)/shard_map/all_gather | solution.py:118
  127.7 15.8 %gather_fusion = f32[4096,4]{1,0:T(8,128)} fusion(f32[4,4096]{0,1:T(8,128)} %all_gather.3, s32[4096]{0:T(1024)S(1)} %broadcast_clamp_fusion), kind=kCustom, calls=%fused_computation.2 | custom fusion | bytes 147456 | tf_op jit(solution)/shard_map/jit(_take)/gather | solution.py:119
  157.0 8.8 %copy.35 = f32[18,4,8,1024]{0,2,3,1:T(8,128)} copy(f32[18,4,8,1024]{3,0,2,1:T(8,128)S(1)} %bitcast.69) | data formatting | bytes 4718592 | tf_op jit(solution)/shard_map/all_to_all | solution.py:132
  165.8 36.9 %gather_fusion.1 = f32[4096,18,8]{1,2,0:T(8,128)} fusion(f32[18,8,4096]{0,1,2:T(8,128)} %bitcast.67, s32[4096]{0:T(1024)} %fusion.32), kind=kCustom, calls=%fused_computation.clone | custom fusion | bytes 4734976 | tf_op jit(solution)/shard_map/jit(_take)/gather | solution.py:133
  202.7 17.0 %broadcast_select_fusion = f32[4096,18,8]{1,2,0:T(8,128)} fusion(f32[4096,18,8]{1,2,0:T(8,128)} %gather_fusion.1, pred[4096]{0:T(1024)(128)(4,1)S(1)} %copy-done.15), kind=kLoop, calls=%fused_computation.5 | loop fusion | flops 589824 | bytes 4722688 | tf_op jit(solution)/shard_map/jit(_take)/select_n | solution.py:133
  219.7 10.4 %copy.38 = f32[18,8,16,256]{3,1,2,0:T(8,128)S(1)} copy(f32[18,8,16,256]{0,1,3,2:T(8,128)} %bitcast.61) | data formatting | bytes 4718592 | tf_op jit(solution)/shard_map/reshape | solution.py:133
  236.2 4.4 collective-permute-done.3
  240.7 6.1 %fusion.10 = f32[18,8,16,256]{3,1,2,0:T(8,128)S(1)} fusion(f32[18,8,16,256]{3,1,2,0:T(8,128)} %copy-done, f32[18,8,1,256]{3,1,2,0:T(8,128)S(1)} %collective-permute-done.3, f32[18,8,1,256]{3,1,2,0:T(8,128)S(1)} %collective-permute-done.2, f32[16,256]{1,0:T(8,128)S(1)} %convert_element_type.20, f32[18,8]{1,0:T(8,128)S(1)} %copy-done.7, ...), kind=kLoop, calls=%fused_computation.37 | loop fusion | flops 8847360 | bytes 5032192 | tf_op jit(solution)/shard_map/mul | solution.py:72
  247.3 4.9 %collective-permute-start.4 = (f32[18,1,4096]{2,1,0:T(1,128)S(1)}, f32[18,1,4096]{2,1,0:T(1,128)}, u32[]{:S(2)}, u32[]{:S(2)}) collective-permute-start(f32[18,1,4096]{2,1,0:T(1,128)S(1)} %get-tuple-element.32), channel_id=1, source_target_pairs={{0,4},{4,8},{8,12},{1,5},{5,9},{9,13},{2,6},{6,10},{10,14},{3,7},{... | collective-permute-start | bytes 884744 | tf_op jit(solution)/shard_map/ppermute | solution.py:54
  253.0 16.2 %scatter_custom_fusion = s32[4096]{0:T(1024)} fusion(s32[4096]{0:T(1024)} %bitcast.77, s32[4096]{0:T(1024)S(1)} %iota.19, s32[]{:T(128)} %constant.33.clone.1), kind=kCustom, calls=%fused_computation.99 | custom fusion | bytes 16896 | tf_op jit(solution)/shard_map/scatter | solution.py:106
  273.1 4.7 collective-permute-done.5
  282.9 5.5 %multiply_add_fusion.1 = f32[18,8,4096]{2,1,0:T(8,128)S(1)} fusion(f32[18,8,4096]{2,1,0:T(8,128)S(1)} %bitcast.66, f32[18,8,4096]{2,0,1:T(8,128)S(1)} %get-tuple-element.20, f32[18,8,4096]{2,0,1:T(8,128)S(1)} %get-tuple-element.23, f32[18,8,4096]{2,0,1:T(8,128)S(1)} %get-tuple-element.24, f32[18,8,4096]{2,0,1:T(8,128)S(1)} %get-tuple-element.19, ...), kind=kLoop, calls=%fused_computation.62 | loop fusion | flops 9437184 | bytes 14581792 | tf_op jit(solution)/shard_map/add | solution.py:143
  293.5 4.1 collective-permute-done.9
  299.4 9.0 %copy.55 = f32[18,8,16,256]{0,1,3,2:T(8,128)} copy(f32[18,8,16,256]{3,1,2,0:T(8,128)S(1)} %fusion.19) | data formatting | bytes 4718592 | tf_op jit(solution)/shard_map/mul | solution.py:72
  308.4 36.8 %gather_fusion.2 = f32[4096,18,8]{1,2,0:T(8,128)} fusion(f32[18,8,4096]{0,1,2:T(8,128)} %bitcast.68, s32[4096]{0:T(1024)S(1)} %copy-done.11), kind=kCustom, calls=%fused_computation.1.clone | custom fusion | bytes 4734976 | tf_op jit(solution)/shard_map/jit(_take)/gather | solution.py:145
  345.1 17.0 %fusion.42 = f32[4096,8,18]{2,1,0:T(8,128)} fusion(f32[4096,18,8]{1,2,0:T(8,128)} %gather_fusion.2, pred[4096]{0:T(1024)(128)(4,1)S(1)} %compare_and_fusion), kind=kLoop, calls=%fused_computation.121 | loop fusion | flops 589824 | bytes 4722688
  362.1 19.8 %reshape.600 = f32[4,1,147456]{2,1,0:T(1,128)S(1)} reshape(f32[4096,8,18]{2,1,0:T(8,128)} %fusion.42) | data formatting | bytes 4718592
  381.9 56.8 %all_to_all.33 = f32[4,1,147456]{2,1,0:T(1,128)} all-to-all(f32[4,1,147456]{2,1,0:T(1,128)S(1)} %reshape.600), channel_id=1, replica_groups=mesh['members'=2,'cards'=4,'sub'=2,'rep'=2] {'cards'}, dimensions={0} | all-to-all | bytes 4718592 | tf_op jit(solution)/shard_map/all_to_all | solution.py:146
  439.2 8.1 %reduce.22 = f32[4,147456]{1,0:T(4,128)S(1)} reduce(f32[4,1,147456]{2,1,0:T(1,128)} %all_to_all.33, f32[]{:T(128)} %broadcast.482), dimensions={1}, to_apply=%all_to_all.28.reduce_sub_computation | reduce | bytes 4718596 | tf_op jit(solution)/shard_map/all_to_all | solution.py:146
  447.3 25.4 %reshape.601 = f32[4096,8,18]{2,1,0:T(8,128)} reshape(f32[4,147456]{1,0:T(4,128)S(1)} %reduce.22) | data formatting | bytes 4718592
  472.7 10.8 %copy.59 = f32[18,8,4,1024]{3,2,1,0:T(4,128)S(1)} copy(f32[18,8,4,1024]{0,1,3,2:T(8,128)} %bitcast.60) | data formatting | bytes 4718592 | tf_op jit(solution)/shard_map/all_to_all | solution.py:146
  485.4 3.8 copy.58
  (128 shorter events, 52.3 us)
Async XLA Ops:
  1.0 9.5 %collective-permute-start = (f32[1,32,1024]{2,0,1:T(1,128)S(1)}, f32[1,32,1024]{2,0,1:T(1,128)S(1)}, u32[]{:S(2)}, u32[]{:S(2)}) collective-permute-start(f32[1,32,1024]{2,0,1:T(1,128)S(1)} %get-tuple-element.36), channel_id=1, source_target_pairs={{1,0},{0,1},{3,2},{2,3},{5,4},{4,5},{7,6},{6,7},{9,8},{8,9},{11,10... | collective-permute-start | bytes 393224 | tf_op jit(solution)/shard_map/ppermute | solution.py:25
  1.5 9.0 %collective-permute-start.1 = (f32[1,32,1024]{2,0,1:T(1,128)S(1)}, f32[1,32,1024]{2,0,1:T(1,128)S(1)}, u32[]{:S(2)}, u32[]{:S(2)}) collective-permute-start(f32[1,32,1024]{2,0,1:T(1,128)S(1)} %get-tuple-element.35), channel_id=1, source_target_pairs={{0,1},{1,0},{2,3},{3,2},{4,5},{5,4},{6,7},{7,6},{8,9},{9,8},{10,11... | collective-permute-start | bytes 393224 | tf_op jit(solution)/shard_map/ppermute | solution.py:22
  5.2 122.5 %copy-start.13 = (s32[4096,1]{0,1:T(1,128)}, s32[4096,1]{0,1:T(1,128)S(1)}, u32[]{:S(2)}) copy-start(s32[4096,1]{0,1:T(1,128)S(1)} %compare_select_fusion) | copy-start | bytes 49156
  5.4 19.8 %copy-start.27 = (f32[18]{0:T(128)}, f32[18]{0:T(128)S(1)}, u32[]{:S(2)}) copy-start(f32[18]{0:T(128)S(1)} %get-tuple-element.18) | copy-start | bytes 220
  18.0 138.9 %all-to-all-start = ((f32[18,32,1024]{2,0,1:T(8,128)}), f32[18,32,1024]{2,0,1:T(8,128)S(1)}, u32[]{:S(2)}, u32[]{:S(2)}) async-start(f32[18,32,1024]{2,0,1:T(8,128)} %multiply_add_fusion), calls=%async_computation | async-start | bytes 6291456 | tf_op jit(solution)/shard_map/all_to_all | solution.py:132
  24.4 119.0 %copy-start.25 = (f32[4,32]{1,0:T(4,128)S(1)}, f32[4,32]{1,0:T(4,128)}, u32[]{:S(2)}) copy-start(f32[4,32]{1,0:T(4,128)} %param.17) | copy-start | bytes 1540
  24.4 119.7 %copy-start.1 = (s32[1,4096]{1,0:T(1,128)S(1)}, s32[1,4096]{1,0:T(1,128)}, u32[]{:S(2)}) copy-start(s32[1,4096]{1,0:T(1,128)} %param.11) | copy-start | bytes 49156
  165.8 36.9 %copy-start.15 = (pred[4096]{0:T(1024)(128)(4,1)S(1)}, pred[4096]{0:T(1024)(128)(4,1)}, u32[]{:S(2)}) copy-start(pred[4096]{0:T(1024)(128)(4,1)} %copy-done.14) | copy-start | bytes 12292
  219.6 15.2 %copy-start.26 = (f32[4,8]{1,0:T(4,128)S(1)}, f32[4,8]{1,0:T(4,128)}, u32[]{:S(2)}) copy-start(f32[4,8]{1,0:T(4,128)} %constant_dynamic-slice_fusion) | copy-start | bytes 388
  219.7 20.9 %copy-start.3 = (f32[18,8]{1,0:T(8,128)S(1)}, f32[18,8]{1,0:T(8,128)}, u32[]{:S(2)}) copy-start(f32[18,8]{1,0:T(8,128)} %get-tuple-element.45) | copy-start | bytes 1732
  219.7 20.9 %copy-start.5 = (f32[18,8]{1,0:T(8,128)S(1)}, f32[18,8]{1,0:T(8,128)}, u32[]{:S(2)}) copy-start(f32[18,8]{1,0:T(8,128)} %get-tuple-element.46) | copy-start | bytes 1732
  219.7 20.9 %copy-start.7 = (f32[18,8]{1,0:T(8,128)S(1)}, f32[18,8]{1,0:T(8,128)}, u32[]{:S(2)}) copy-start(f32[18,8]{1,0:T(8,128)} %get-tuple-element.49) | copy-start | bytes 1732
  219.7 20.9 %copy-start.9 = (f32[18,8]{1,0:T(8,128)S(1)}, f32[18,8]{1,0:T(8,128)}, u32[]{:S(2)}) copy-start(f32[18,8]{1,0:T(8,128)} %get-tuple-element.50) | copy-start | bytes 1732
  230.1 6.1 %collective-permute-start.2 = (f32[18,8,1,256]{3,1,2,0:T(8,128)S(1)}, f32[18,8,1,256]{3,1,2,0:T(8,128)S(1)}, u32[]{:S(2)}, u32[]{:S(2)}) collective-permute-start(f32[18,8,1,256]{3,1,2,0:T(8,128)S(1)} %get-tuple-element.33), channel_id=1, source_target_pairs={{0,2},{1,3},{4,6},{5,7},{8,10},{9,11},{12,14},{13,15},{16,18},{17,... | collective-permute-start | bytes 442376 | tf_op jit(solution)/shard_map/ppermute | solution.py:22
  233.5 7.0 %collective-permute-start.3 = (f32[18,8,1,256]{3,1,2,0:T(8,128)S(1)}, f32[18,8,1,256]{3,1,2,0:T(8,128)S(1)}, u32[]{:S(2)}, u32[]{:S(2)}) collective-permute-start(f32[18,8,1,256]{3,1,2,0:T(8,128)S(1)} %get-tuple-element.34), channel_id=1, source_target_pairs={{2,0},{3,1},{6,4},{7,5},{10,8},{11,9},{14,12},{15,13},{18,16},{19,... | collective-permute-start | bytes 442376 | tf_op jit(solution)/shard_map/ppermute | solution.py:25
  247.3 23.2 %collective-permute-start.4 = (f32[18,1,4096]{2,1,0:T(1,128)S(1)}, f32[18,1,4096]{2,1,0:T(1,128)}, u32[]{:S(2)}, u32[]{:S(2)}) collective-permute-start(f32[18,1,4096]{2,1,0:T(1,128)S(1)} %get-tuple-element.32), channel_id=1, source_target_pairs={{0,4},{4,8},{8,12},{1,5},{5,9},{9,13},{2,6},{6,10},{10,14},{3,7},{... | collective-permute-start | bytes 884744 | tf_op jit(solution)/shard_map/ppermute | solution.py:54
  269.2 8.6 %collective-permute-start.5 = (f32[18,1,4096]{2,1,0:T(1,128)S(1)}, f32[18,1,4096]{2,1,0:T(1,128)S(1)}, u32[]{:S(2)}, u32[]{:S(2)}) collective-permute-start(f32[18,1,4096]{2,1,0:T(1,128)S(1)} %get-tuple-element.31), channel_id=1, source_target_pairs={{4,0},{8,4},{12,8},{5,1},{9,5},{13,9},{6,2},{10,6},{14,10},{7,3},{... | collective-permute-start | bytes 884744 | tf_op jit(solution)/shard_map/ppermute | solution.py:55
  278.3 1.5 collective-permute-start.6
  278.3 1.6 collective-permute-start.7
  282.8 14.8 %copy-start.4 = (f32[18,8]{1,0:T(8,128)S(1)}, f32[18,8]{1,0:T(8,128)}, u32[]{:S(2)}) copy-start(f32[18,8]{1,0:T(8,128)} %get-tuple-element.45) | copy-start | bytes 1732
  282.8 14.8 %copy-start.6 = (f32[18,8]{1,0:T(8,128)S(1)}, f32[18,8]{1,0:T(8,128)}, u32[]{:S(2)}) copy-start(f32[18,8]{1,0:T(8,128)} %get-tuple-element.46) | copy-start | bytes 1732
  282.8 14.8 %copy-start.8 = (f32[18,8]{1,0:T(8,128)S(1)}, f32[18,8]{1,0:T(8,128)}, u32[]{:S(2)}) copy-start(f32[18,8]{1,0:T(8,128)} %get-tuple-element.49) | copy-start | bytes 1732
  288.4 5.1 %collective-permute-start.8 = (f32[18,8,1,256]{3,1,2,0:T(8,128)S(1)}, f32[18,8,1,256]{3,1,2,0:T(8,128)S(1)}, u32[]{:S(2)}, u32[]{:S(2)}) collective-permute-start(f32[18,8,1,256]{3,1,2,0:T(8,128)S(1)} %get-tuple-element.29), channel_id=1, source_target_pairs={{0,2},{1,3},{4,6},{5,7},{8,10},{9,11},{12,14},{13,15},{16,18},{17,... | collective-permute-start | bytes 442376 | tf_op jit(solution)/shard_map/ppermute | solution.py:22
  289.9 7.8 %collective-permute-start.9 = (f32[18,8,1,256]{3,1,2,0:T(8,128)S(1)}, f32[18,8,1,256]{3,1,2,0:T(8,128)S(1)}, u32[]{:S(2)}, u32[]{:S(2)}) collective-permute-start(f32[18,8,1,256]{3,1,2,0:T(8,128)S(1)} %get-tuple-element.30), channel_id=1, source_target_pairs={{2,0},{3,1},{6,4},{7,5},{10,8},{11,9},{14,12},{15,13},{18,16},{19,... | collective-permute-start | bytes 442376 | tf_op jit(solution)/shard_map/ppermute | solution.py:25
  (19 other events, 154.2 us)

commit v2 on v0

v2 whole, which is shorter than its diff:
```python
import functools

import jax
import jax.numpy as jnp
from jax import lax
from jax.experimental import pallas as pl
from jax.experimental.pallas import tpu as pltpu
from jax.sharding import PartitionSpec as P

F0 = 0.035
GROWTH = 1.1
CNL = 0.25
COURANT = 0.6
MESH = pl.DeviceIdType.MESH


def nonlinear(energy, pone, mone, ptwo, mtwo):
    return CNL * (
        energy * energy * (pone + mone + ptwo + mtwo) - 2.0 * energy * (pone * mone + ptwo * mtwo)
    )


def rate_of(cols, classes, root, class_count):
    rate = jnp.zeros((cols.shape[0], classes.shape[1]), jnp.float32)
    for k in range(class_count):
        rate = jnp.where(jnp.abs(classes - k) < 0.5, cols[:, k : k + 1], rate)
    return rate * root


def kernel(
    sizes, x, slot, marks, pts, ang, fall, fown, out,
    halo, send, recv, precv, lhs, acc, g, flo, fhi, elo, ehi, rows1, rows2,
    rate1, rate2, mv, lhs2, sback, rback, ssem, rsem,
):
    dirs, freqs, points, n, own, ns, nrep, classes, cols = sizes
    cells = n * points
    comp = dirs * own
    pad = send.shape[1]
    me = lax.axis_index("cards")
    sub = lax.axis_index("sub")
    rep = lax.axis_index("rep")
    rep_next, rep_prev = lax.rem(rep + 1, nrep), lax.rem(rep + nrep - 1, nrep)
    sub_next, sub_prev = lax.rem(sub + 1, ns), lax.rem(sub + ns - 1, ns)

    barrier = pltpu.get_barrier_semaphore()

    def greet(o, carry):
        pl.semaphore_signal(
            barrier, inc=1, device_id={"cards": lax.rem(me + o, n)}, device_id_type=MESH
        )
        return carry

    lax.fori_loop(1, n, greet, 0)
    for name, other in (("rep", rep_next), ("rep", rep_prev), ("sub", sub_next), ("sub", sub_prev)):
        pl.semaphore_signal(barrier, inc=1, device_id={name: other}, device_id_type=MESH)
    pl.semaphore_wait(barrier, n - 1 + 4)

    def copy(src, dst, sem, name, other):
        return pltpu.make_async_remote_copy(
            src_ref=src, dst_ref=dst, send_sem=ssem.at[sem], recv_sem=rsem.at[sem],
            device_id={name: other}, device_id_type=MESH,
        )

    REP1, SUB1, SUB2, FRQ, REP2, PAR = 0, 2, 4, 6, 8, 14
    AIN = PAR + n
    AOUT = AIN + n

    rep1 = [
        copy(x.at[0], halo.at[1], REP1, "rep", rep_prev),
        copy(x.at[dirs - 1], halo.at[0], REP1 + 1, "rep", rep_next),
    ]
    for c in rep1:
        c.start()

    def par_copy(o):
        return copy(pts, precv.at[me], PAR + o, "cards", lax.rem(me + o, n))

    def in_copy(o):
        to = lax.rem(me + o, n)
        return copy(send.at[to], recv.at[me], AIN + o, "cards", to)

    def out_copy(o):
        to = lax.rem(me + o, n)
        return copy(sback.at[to], rback.at[me], AOUT + o, "cards", to)

    def each(first, last, body):
        def step(i, carry):
            body(i)
            return carry

        lax.fori_loop(first, last, step, 0)

    each(1, n, lambda o: par_copy(o).start())

    rate1[...] = rate_of(fall, pts[2:3, :], pts[3:4, :], classes)
    lane = min(256, points)

    def source1(d, plus, minus):
        def tile(t):
            at = pl.ds(pl.multiple_of(t * lane, lane), lane)
            row = lax.broadcasted_iota(jnp.int32, (freqs, lane), 0)

            def up(v):
                return jnp.where(row == freqs - 1, 0.0, pltpu.roll(v, freqs - 1, 0))

            def down(v):
                return jnp.where(row == 0, 0.0, pltpu.roll(v, 1, 0))

            e, p, m = x[d, :, at], plus(at), minus(at)
            beta = jnp.maximum(ang[0, d] * pts[0:1, at] + ang[1, d] * pts[1:2, at], 0.0)
            grow = jnp.exp(beta * fall[:, classes : classes + 1] - rate1[:, at])
            s = e * grow + nonlinear(e, up(p), down(m), up(m), down(p))
            for k in range(n):
                send[k, pl.ds(pl.multiple_of(d * own, own), own), at] = s[k * own : (k + 1) * own]

        each(0, points // lane, tile)

    each(1, dirs - 1, lambda d: source1(d, lambda at: x[d + 1, :, at], lambda at: x[d - 1, :, at]))
    for c in rep1:
        c.wait_recv()
    source1(0, lambda at: x[1, :, at], lambda at: halo[0, :, at])
    source1(dirs - 1, lambda at: halo[1, :, at], lambda at: x[dirs - 2, :, at])
    each(1, n, lambda o: in_copy(o).start())

    half = pad + 8
    width = min(512, cells)

    def gather_in(values, params, frm, first):
        v = jnp.concatenate([values, params], axis=0)
        low = v - v.astype(jnp.bfloat16).astype(jnp.float32)
        lhs[...] = jnp.concatenate([v, low], axis=0).astype(jnp.bfloat16)

        def tile(t):
            at = pl.ds(pl.multiple_of(t * width, width), width)
            point = lax.broadcasted_iota(jnp.int32, (points, width), 0)
            hot = jnp.where(point == slot[:, at] - frm * points, 1.0, 0.0).astype(jnp.bfloat16)
            r = jnp.dot(lhs[...], hot, preferred_element_type=jnp.float32)
            r = r[:half] + r[half:]
            if first:
                acc[:, at] = r
            else:
                acc[:, at] += r

        each(0, cells // width, tile)

    gather_in(send[me], pts[...], me, True)

    def arrived(o):
        frm = lax.rem(me + n - o, n)
        par_copy(o).wait_recv()
        in_copy(o).wait_recv()
        gather_in(recv[frm], precv[frm], frm, False)

    each(1, n, arrived)

    def row_copies(rows, sem):
        last = pl.ds(cells - cols, cols)
        return (
            copy(acc.at[pl.ds(0, pad), last], rows.at[0], sem, "sub", sub_next),
            copy(acc.at[pl.ds(0, pad), pl.ds(0, cols)], rows.at[1], sem + 1, "sub", sub_prev),
        )

    def start_rows(rows, sem):
        to_next, to_prev = row_copies(rows, sem)

        @pl.when(sub < ns - 1)
        def _():
            to_next.start()

        @pl.when(sub > 0)
        def _():
            to_prev.start()

    def recv_rows(rows, sem):
        to_next, to_prev = row_copies(rows, sem)

        @pl.when(sub > 0)
        def _():
            to_next.wait_recv()

        @pl.when(sub == 0)
        def _():
            rows[0] = jnp.zeros((pad, cols), jnp.float32)

        @pl.when(sub < ns - 1)
        def _():
            to_prev.wait_recv()

        @pl.when(sub == ns - 1)
        def _():
            rows[1] = jnp.zeros((pad, cols), jnp.float32)

    def sent_rows(rows, sem):
        to_next, to_prev = row_copies(rows, sem)

        @pl.when(sub < ns - 1)
        def _():
            to_next.wait_send()

        @pl.when(sub > 0)
        def _():
            to_prev.wait_send()

    def moved(d, rows):
        at = pl.ds(pl.multiple_of(d * own, own), own)
        e = acc[at, :]
        below = jnp.concatenate([rows[0, at, :], e[:, : cells - cols]], axis=1)
        above = jnp.concatenate([e[:, cols:], rows[1, at, :]], axis=1)
        left = pltpu.roll(e, 1, 1) * marks[1:2, :]
        right = pltpu.roll(e, cells - 1, 1) * marks[2:3, :]
        speed = fown[:, classes + 1 : classes + 2]
        nux, nuy = ang[0, d] * speed, ang[1, d] * speed
        m = (
            e
            - jnp.maximum(nux, 0.0) * (e - left)
            - jnp.minimum(nux, 0.0) * (right - e)
            - jnp.maximum(nuy, 0.0) * (e - below)
            - jnp.minimum(nuy, 0.0) * (above - e)
        )
        return m * marks[0:1, :]

    start_rows(rows1, SUB1)
    rate2[...] = rate_of(fown, acc[pad + 2 : pad + 3, :], acc[pad + 3 : pad + 4, :], classes)
    recv_rows(rows1, SUB1)

    def prop1(d):
        m = moved(d, rows1)
        g[d + 1] = m
        elo[d] = m[0:1]
        ehi[d] = m[own - 1 : own]

    each(0, dirs, prop1)

    inner = pl.ds(1, dirs)
    rep2 = [
        copy(g.at[1], g.at[dirs + 1], REP2, "rep", rep_prev),
        copy(g.at[dirs], g.at[0], REP2 + 1, "rep", rep_next),
        copy(flo.at[1], flo.at[dirs + 1], REP2 + 2, "rep", rep_prev),
        copy(flo.at[dirs], flo.at[0], REP2 + 3, "rep", rep_next),
        copy(fhi.at[1], fhi.at[dirs + 1], REP2 + 4, "rep", rep_prev),
        copy(fhi.at[dirs], fhi.at[0], REP2 + 5, "rep", rep_next),
    ]
    to_upper = copy(ehi, flo.at[inner], FRQ, "cards", lax.rem(me + 1, n))
    to_lower = copy(elo, fhi.at[inner], FRQ + 1, "cards", lax.rem(me + n - 1, n))

    @pl.when(me < n - 1)
    def _():
        to_upper.start()

    @pl.when(me > 0)
    def _():
        to_lower.start()

    rep2[0].start()
    rep2[1].start()
    sent_rows(rows1, SUB1)

    @pl.when(me > 0)
    def _():
        to_upper.wait_recv()

    @pl.when(me == 0)
    def _():
        flo[inner] = jnp.zeros((dirs, 1, cells), jnp.float32)

    @pl.when(me < n - 1)
    def _():
        to_lower.wait_recv()

    @pl.when(me == n - 1)
    def _():
        fhi[inner] = jnp.zeros((dirs, 1, cells), jnp.float32)

    for c in rep2[2:]:
        c.start()

    span = min(1024, cells)

    def source2(d):
        def tile(t):
            at = pl.ds(pl.multiple_of(t * span, span), span)
            row = lax.broadcasted_iota(jnp.int32, (own, span), 0)

            def up(i):
                edge = jnp.broadcast_to(fhi[i, :, at], (own, span))
                if own == 1:
                    return edge
                return jnp.where(row == own - 1, edge, pltpu.roll(g[i, :, at], own - 1, 0))

            def down(i):
                edge = jnp.broadcast_to(flo[i, :, at], (own, span))
                if own == 1:
                    return edge
                return jnp.where(row == 0, edge, pltpu.roll(g[i, :, at], 1, 0))

            e = g[d + 1, :, at]
            a, b = acc[pad : pad + 1, at], acc[pad + 1 : pad + 2, at]
            beta = jnp.maximum(ang[0, d] * a + ang[1, d] * b, 0.0)
            grow = jnp.exp(beta * fown[:, classes : classes + 1] - rate2[:, at])
            acc[pl.ds(pl.multiple_of(d * own, own), own), at] = e * grow + nonlinear(
                e, up(d + 2), down(d), up(d), down(d + 2)
            )

        each(0, cells // span, tile)

    each(1, dirs - 1, source2)
    for c in rep2:
        c.wait_recv()
    source2(0)
    source2(dirs - 1)

    start_rows(rows2, SUB2)
    recv_rows(rows2, SUB2)

    def prop2(d):
        mv[pl.ds(pl.multiple_of(d * own, own), own), :] = moved(d, rows2)

    each(0, dirs, prop2)

    block = min(512, cells)

    def split(t):
        at = pl.ds(pl.multiple_of(t * block, block), block)
        v = mv[:, at]
        low = v - v.astype(jnp.bfloat16).astype(jnp.float32)
        lhs2[:, at] = jnp.concatenate([v, low], axis=0).astype(jnp.bfloat16)

    each(0, cells // block, split)
    tall = min(256, points)

    def gather_out(to, dst):
        def tile(t):
            base = to * points + t * tall
            point = lax.broadcasted_iota(jnp.int32, (tall, cells), 0)
            hot = jnp.where(point == slot[...] - base, 1.0, 0.0).astype(jnp.bfloat16)
            r = lax.dot_general(
                lhs2[...], hot, (((1,), (1,)), ((), ())), preferred_element_type=jnp.float32
            )
            dst[to, :, pl.ds(pl.multiple_of(t * tall, tall), tall)] = r[:pad] + r[pad:]

        each(0, points // tall, tile)

    def leave(o):
        gather_out(lax.rem(me + o, n), sback)
        out_copy(o).start()

    each(1, n, leave)
    gather_out(me, rback)

    def place(frm):
        for d in range(dirs):
            out[d, pl.ds(pl.multiple_of(frm * own, own), own), :] = rback[
                frm, d * own : (d + 1) * own, :
            ]

    place(me)

    def back(o):
        out_copy(o).wait_recv()
        place(lax.rem(me + n - o, n))

    each(1, n, back)

    for c in rep1 + rep2:
        c.wait_send()

    @pl.when(me < n - 1)
    def _():
        to_upper.wait_send()

    @pl.when(me > 0)
    def _():
        to_lower.wait_send()

    sent_rows(rows2, SUB2)

    def gone(o):
        par_copy(o).wait_send()
        in_copy(o).wait_send()
        out_copy(o).wait_send()

    each(1, n, gone)


def shards(spectra, deal_slot, sea_mask, ice_class, brine, wind_rate, wind_dir, ice_table):
    dirs, freqs, _, points = spectra.shape
    n = lax.axis_size("cards")
    me = lax.axis_index("cards")
    ns = lax.axis_size("sub")
    nrep = lax.axis_size("rep")
    rep = lax.axis_index("rep")
    own = freqs // n
    rows, cols = sea_mask.shape
    cells = rows * cols
    classes = ice_table.shape[0]
    comp = dirs * own
    pad = -(-comp // 8) * 8

    theta = 2.0 * jnp.pi * jnp.arange(dirs * nrep, dtype=jnp.float32) / (dirs * nrep)
    theta = lax.dynamic_slice_in_dim(theta, rep * dirs, dirs, 0)
    ang = jnp.stack([jnp.cos(theta), jnp.sin(theta)])
    freq = F0 * GROWTH ** jnp.arange(freqs, dtype=jnp.float32)
    fall = jnp.concatenate(
        [ice_table.T, (freq / freq[-1])[:, None], (COURANT * (freq[0] / freq))[:, None]], axis=1
    )
    fown = lax.dynamic_slice_in_dim(fall, me * own, own, 0)
    wave = wind_rate[0]
    point_rows = [
        wave * jnp.cos(wind_dir[0]),
        wave * jnp.sin(wind_dir[0]),
        ice_class[0].astype(jnp.float32),
        jnp.sqrt(brine[0] / 0.1),
    ]
    pts = jnp.stack(point_rows + [jnp.zeros_like(wave)] * 4)
    col = lax.broadcasted_iota(jnp.int32, (rows, cols), 1).reshape(-1)
    marks = jnp.stack(
        [
            sea_mask.reshape(-1).astype(jnp.float32),
            (col != 0).astype(jnp.float32),
            (col != cols - 1).astype(jnp.float32),
        ]
    )
    f32 = jnp.float32
    vmem = pltpu.VMEM
    count = 14 + 3 * n
    sizes = (dirs, freqs, points, n, own, ns, nrep, classes, cols)
    spec = pl.BlockSpec(memory_space=pltpu.VMEM)
    result = pl.pallas_call(
        functools.partial(kernel, sizes),
        out_shape=jax.ShapeDtypeStruct((dirs, freqs, points), f32),
        in_specs=[spec] * 4 + [pl.BlockSpec(memory_space=pltpu.SMEM)] + [spec] * 2,
        out_specs=spec,
        scratch_shapes=[
            vmem((2, freqs, points), f32),
            vmem((n, pad, points), f32),
            vmem((n, pad, points), f32),
            vmem((n, 8, points), f32),
            vmem((2 * (pad + 8), points), jnp.bfloat16),
            vmem((pad + 8, cells), f32),
            vmem((dirs + 2, own, cells), f32),
            vmem((dirs + 2, 1, cells), f32),
            vmem((dirs + 2, 1, cells), f32),
            vmem((dirs, 1, cells), f32),
            vmem((dirs, 1, cells), f32),
            vmem((2, pad, cols), f32),
            vmem((2, pad, cols), f32),
            vmem((freqs, points), f32),
            vmem((own, cells), f32),
            vmem((pad, cells), f32),
            vmem((2 * pad, cells), jnp.bfloat16),
            vmem((n, pad, points), f32),
            vmem((n, pad, points), f32),
            pltpu.SemaphoreType.DMA((count,)),
            pltpu.SemaphoreType.DMA((count,)),
        ],
        compiler_params=pltpu.CompilerParams(
            collective_id=0, has_side_effects=True, vmem_limit_bytes=56 * 2**20
        ),
    )(spectra.reshape(dirs, freqs, points), deal_slot, marks, pts, ang, fall, fown)
    return result[:, :, None, :]


def solution(mesh):
    placed = (
        P("rep", None, "sub", ("members", "cards")),
        P("sub", "members"),
        P("sub", "members"),
        P("sub", ("members", "cards")),
        P("sub", ("members", "cards")),
        P("sub", ("members", "cards")),
        P("sub", ("members", "cards")),
        P(),
    )
    return jax.shard_map(
        shards,
        mesh=mesh,
        in_specs=placed,
        out_specs=P("rep", None, "sub", ("members", "cards")),
        check_vma=False,
    )
```

time: 543 us -> 166 us (0.31)
  the two profiles are of different devices: /device:TPU:0 before, /device:TPU:11 now
where the time goes in v2:
time: 166 us
  Pallas kernels  149 us (90%)
  local copies, waits for them, and re-layouts  11.3 us (7%)
  other arithmetic  5.54 us (3%)
    pallas_call x1, Pallas kernels, shards(): pl.pallas_call(functools.partial(kernel, sizes), out_shape=jax.ShapeDtype...  149 us
    broadcast_in_dim x1, local copies, waits for them, and re-layouts, shards(): return result[:, :, None, :]  5.6 us
    unnamed x6, local copies, waits for them, and re-layouts  3.67 us

profile of v2, /device:TPU:11, one launch (start us, length us, event | category | flops | bytes accessed | tf_op | source)
XLA Modules:
  0.0 165.8 jit_solution(15845741560444553916)
XLA Ops:
  0.0 0.1 cosine_bitcast_fusion
  0.1 0.6 pad_maximum_fusion.2.ang
  0.7 0.6 fusion.1
  1.3 1.3 divide_multiply_fusion
  2.6 0.7 pad_maximum_fusion.1
  3.3 0.7 convert_element_type.49
  4.0 0.1 copy.12.fall
  4.1 0.0 copy-start
  4.1 0.6 constant_dynamic-slice_fusion.fown
  4.7 0.9 sine_multiply_fusion
  5.5 0.7 convert_bitcast_fusion.2
  6.3 0.6 stack.27.pts
  7.0 0.7 pad_maximum_fusion.marks
  7.7 3.6 %copy.19 = f32[18,32,1,1024]{3,1,2,0:T(8,128)} copy(f32[18,32,1,1024]{3,2,1,0:T(1,128)} %param.8) | data formatting | bytes 4718592
  11.3 0.0 copy-done
  11.3 148.9 %shard_map.82 = f32[18,32,1024]{2,1,0:T(8,128)} custom-call(f32[18,32,1024]{2,1,0:T(8,128)} %bitcast.24, s32[1,4096]{1,0:T(1,128)} %slot.1, f32[3,4096]{1,0:T(4,128)} %pad_maximum_fusion.marks, f32[8,1024]{1,0:T(8,128)} %stack.27.pts, f32[2,18]{1,0:T(2,128)} %pad_maximum_fusion.2.ang, f32[32,6]{1,0:T(8,128)} %copy-done, f32[8,6]{1,0:T(8,128)} %constant_dynamic-slice_fusion.fown), custom_call_target="tpu_custom_call" | custom-call | tf_op jit(solution)/shard_map/pallas_call | solution.py:428
  160.2 5.6 %copy.13 = f32[18,32,1,1024]{3,2,1,0:T(1,128)} copy(f32[18,32,1,1024]{3,1,0,2:T(8,128)} %bitcast.23) | data formatting | bytes 4718592 | tf_op jit(solution)/shard_map/broadcast_in_dim | solution.py:460
  (8 shorter events, 0.1 us)
Async XLA Ops:
  4.1 7.2 %copy-start = (f32[32,6]{1,0:T(8,128)}, f32[32,6]{1,0:T(8,128)S(1)}, u32[]{:S(2)}) copy-start(f32[32,6]{1,0:T(8,128)S(1)} %copy.12.fall) | copy-start | bytes 2308

commit v3 on v2

--- a/solution.py
+++ b/solution.py
@@ -2,6 +2,7 @@
 
 import jax
 import jax.numpy as jnp
+import numpy as np
 from jax import lax
 from jax.experimental import pallas as pl
 from jax.experimental.pallas import tpu as pltpu
@@ -28,11 +29,11 @@
 
 
 def kernel(
-    sizes, x, slot, marks, pts, ang, fall, fown, out,
-    halo, send, recv, precv, lhs, acc, g, flo, fhi, elo, ehi, rows1, rows2,
+    sizes, x, slot, sea, ice_class, brine, wind_rate, wind_dir, ang_all, fall, out,
+    marks, pts, ang, fown, halo, send, recv, precv, lhs, acc, g, flo, fhi, elo, ehi, rows1, rows2,
     rate1, rate2, mv, lhs2, sback, rback, ssem, rsem,
 ):
-    dirs, freqs, points, n, own, ns, nrep, classes, cols = sizes
+    dirs, freqs, points, n, own, ns, nrep, classes, grid_rows, cols = sizes
     cells = n * points
     comp = dirs * own
     pad = send.shape[1]
@@ -61,9 +62,13 @@
             device_id={name: other}, device_id_type=MESH,
         )
 
-    REP1, SUB1, SUB2, FRQ, REP2, PAR = 0, 2, 4, 6, 8, 14
+    REP1, SUB1, SUB2, FRQ, REP2, PAR = 0, 2, 4, 6, 14, 20
     AIN = PAR + n
-    AOUT = AIN + n
+    AOUT = AIN + 2 * n
+    tall = min(256, points)
+    tiles = points // tall
+    cut = (dirs // 2) * own
+    cuts = ((0, cut), (cut, pad)) if cut % 8 == 0 else ((0, pad),)
 
     rep1 = [
         copy(x.at[0], halo.at[1], REP1, "rep", rep_prev),
@@ -75,13 +80,18 @@
     def par_copy(o):
         return copy(pts, precv.at[me], PAR + o, "cards", lax.rem(me + o, n))
 
-    def in_copy(o):
+    def in_copy(o, part):
         to = lax.rem(me + o, n)
-        return copy(send.at[to], recv.at[me], AIN + o, "cards", to)
-
-    def out_copy(o):
+        first, last = cuts[part]
+        at = pl.ds(first, last - first)
+        return copy(send.at[to, at], recv.at[me, at], AIN + 2 * o + part, "cards", to)
+
+    def out_copy(o, t):
         to = lax.rem(me + o, n)
-        return copy(sback.at[to], rback.at[me], AOUT + o, "cards", to)
+        at = pl.ds(pl.multiple_of(t * tall, tall), tall)
+        return copy(
+            sback.at[to, :, at], rback.at[me, :, at], AOUT + o * tiles + t, "cards", to
+        )
 
     def each(first, last, body):
         def step(i, carry):
@@ -90,7 +100,26 @@
 
         lax.fori_loop(first, last, step, 0)
 
+    wave = wind_rate[...]
+    pts[0:1, :] = wave * jnp.cos(wind_dir[...])
+    pts[1:2, :] = wave * jnp.sin(wind_dir[...])
+    pts[2:3, :] = ice_class[...].astype(jnp.float32)
+    pts[3:4, :] = jnp.sqrt(brine[...] / 0.1)
+    pts[4:8, :] = jnp.zeros((4, points), jnp.float32)
     each(1, n, lambda o: par_copy(o).start())
+
+    def angle(d):
+        ang[0, d] = ang_all[0, rep * dirs + d]
+        ang[1, d] = ang_all[1, rep * dirs + d]
+
+    each(0, dirs, angle)
+    fown[...] = fall[pl.ds(pl.multiple_of(me * own, own), own), :]
+    col = lax.broadcasted_iota(jnp.int32, (1, cols), 1)
+    for r in range(grid_rows):
+        at = slice(r * cols, (r + 1) * cols)
+        marks[0:1, at] = sea[r : r + 1, :].astype(jnp.float32)
+        marks[1:2, at] = jnp.where(col == 0, 0.0, 1.0)
+        marks[2:3, at] = jnp.where(col == cols - 1, 0.0, 1.0)
 
     rate1[...] = rate_of(fall, pts[2:3, :], pts[3:4, :], classes)
     lane = min(256, points)
@@ -106,7 +135,7 @@
             def down(v):
                 return jnp.where(row == 0, 0.0, pltpu.roll(v, 1, 0))
 
-            e, p, m = x[d, :, at], plus(at), minus(at)
+            e, p, m = x[d, :, 0, at], plus(at), minus(at)
             beta = jnp.maximum(ang[0, d] * pts[0:1, at] + ang[1, d] * pts[1:2, at], 0.0)
             grow = jnp.exp(beta * fall[:, classes : classes + 1] - rate1[:, at])
             s = e * grow + nonlinear(e, up(p), down(m), up(m), down(p))
@@ -115,17 +144,25 @@
 
         each(0, points // lane, tile)
 
-    each(1, dirs - 1, lambda d: source1(d, lambda at: x[d + 1, :, at], lambda at: x[d - 1, :, at]))
+    def middle1(d):
+        source1(d, lambda at: x[d + 1, :, 0, at], lambda at: x[d - 1, :, 0, at])
+
+    each(1, dirs // 2, middle1)
     for c in rep1:
         c.wait_recv()
-    source1(0, lambda at: x[1, :, at], lambda at: halo[0, :, at])
-    source1(dirs - 1, lambda at: halo[1, :, at], lambda at: x[dirs - 2, :, at])
-    each(1, n, lambda o: in_copy(o).start())
+    source1(0, lambda at: x[1, :, 0, at], lambda at: halo[0, :, 0, at])
+    if len(cuts) == 2:
+        each(1, n, lambda o: in_copy(o, 0).start())
+    each(dirs // 2, dirs - 1, middle1)
+    source1(dirs - 1, lambda at: halo[1, :, 0, at], lambda at: x[dirs - 2, :, 0, at])
+    each(1, n, lambda o: in_copy(o, len(cuts) - 1).start())
 
     half = pad + 8
     width = min(512, cells)
 
-    def gather_in(values, params, frm, first):
+    count = cells // width
+
+    def gather_in(values, params, frm, first, between=None):
         v = jnp.concatenate([values, params], axis=0)
         low = v - v.astype(jnp.bfloat16).astype(jnp.float32)
         lhs[...] = jnp.concatenate([v, low], axis=0).astype(jnp.bfloat16)
@@ -141,17 +178,14 @@
             else:
                 acc[:, at] += r
 
-        each(0, cells // width, tile)
+        tile(0)
+        if count > 1:
+            tile(count - 1)
+        if between is not None:
+            between()
+        each(1, count - 1, tile)
 
     gather_in(send[me], pts[...], me, True)
-
-    def arrived(o):
-        frm = lax.rem(me + n - o, n)
-        par_copy(o).wait_recv()
-        in_copy(o).wait_recv()
-        gather_in(recv[frm], precv[frm], frm, False)
-
-    each(1, n, arrived)
 
     def row_copies(rows, sem):
         last = pl.ds(cells - cols, cols)
@@ -219,7 +253,16 @@
         )
         return m * marks[0:1, :]
 
-    start_rows(rows1, SUB1)
+    def arrived(o, between=None):
+        frm = lax.rem(me + n - o, n)
+        par_copy(o).wait_recv()
+        for part in range(len(cuts)):
+            in_copy(o, part).wait_recv()
+        gather_in(recv[frm], precv[frm], frm, False, between)
+
+    each(1, n - 1, arrived)
+    arrived(n - 1, lambda: start_rows(rows1, SUB1))
+
     rate2[...] = rate_of(fown, acc[pad + 2 : pad + 3, :], acc[pad + 3 : pad + 4, :], classes)
     recv_rows(rows1, SUB1)
 
@@ -229,7 +272,8 @@
         elo[d] = m[0:1]
         ehi[d] = m[own - 1 : own]
 
-    each(0, dirs, prop1)
+    prop1(0)
+    prop1(dirs - 1)
 
     inner = pl.ds(1, dirs)
     rep2 = [
@@ -240,44 +284,63 @@
         copy(fhi.at[1], fhi.at[dirs + 1], REP2 + 4, "rep", rep_prev),
         copy(fhi.at[dirs], fhi.at[0], REP2 + 5, "rep", rep_next),
     ]
-    to_upper = copy(ehi, flo.at[inner], FRQ, "cards", lax.rem(me + 1, n))
-    to_lower = copy(elo, fhi.at[inner], FRQ + 1, "cards", lax.rem(me + n - 1, n))
-
-    @pl.when(me < n - 1)
-    def _():
-        to_upper.start()
-
-    @pl.when(me > 0)
-    def _():
-        to_lower.start()
-
     rep2[0].start()
     rep2[1].start()
-    sent_rows(rows1, SUB1)
-
-    @pl.when(me > 0)
-    def _():
-        to_upper.wait_recv()
+    upper, lower = lax.rem(me + 1, n), lax.rem(me + n - 1, n)
+    half_dirs = dirs // 2
+    groups = ((0, 1), (dirs - 1, 1), (1, half_dirs - 1), (half_dirs, dirs - 1 - half_dirs))
+    to_upper, to_lower = [], []
+    for i, (first, size) in enumerate(groups):
+        src, dst = pl.ds(first, size), pl.ds(first + 1, size)
+        to_upper.append(copy(ehi.at[src], flo.at[dst], FRQ + 2 * i, "cards", upper))
+        to_lower.append(copy(elo.at[src], fhi.at[dst], FRQ + 2 * i + 1, "cards", lower))
+
+    def start_edges(chosen):
+        @pl.when(me < n - 1)
+        def _():
+            for i in chosen:
+                to_upper[i].start()
+
+        @pl.when(me > 0)
+        def _():
+            for i in chosen:
+                to_lower[i].start()
+
+    def recv_edges(chosen):
+        @pl.when(me > 0)
+        def _():
+            for i in chosen:
+                to_upper[i].wait_recv()
+
+        @pl.when(me < n - 1)
+        def _():
+            for i in chosen:
+                to_lower[i].wait_recv()
 
     @pl.when(me == 0)
     def _():
         flo[inner] = jnp.zeros((dirs, 1, cells), jnp.float32)
 
-    @pl.when(me < n - 1)
-    def _():
-        to_lower.wait_recv()
-
     @pl.when(me == n - 1)
     def _():
         fhi[inner] = jnp.zeros((dirs, 1, cells), jnp.float32)
 
+    start_edges((0, 1))
+    each(1, half_dirs, prop1)
+    start_edges((2,))
+    recv_edges((0, 1))
     for c in rep2[2:]:
         c.start()
+    each(half_dirs, dirs - 1, prop1)
+    start_edges((3,))
+    sent_rows(rows1, SUB1)
 
     span = min(1024, cells)
 
-    def source2(d):
-        def tile(t):
+    spans = cells // span
+
+    def source2(t):
+        def tile(d):
             at = pl.ds(pl.multiple_of(t * span, span), span)
             row = lax.broadcasted_iota(jnp.int32, (own, span), 0)
 
@@ -301,15 +364,17 @@
                 e, up(d + 2), down(d), up(d), down(d + 2)
             )
 
-        each(0, cells // span, tile)
-
-    each(1, dirs - 1, source2)
+        each(0, dirs, tile)
+
     for c in rep2:
         c.wait_recv()
+    recv_edges((2, 3))
     source2(0)
-    source2(dirs - 1)
+    if spans > 1:
+        source2(spans - 1)
 
     start_rows(rows2, SUB2)
+    each(1, spans - 1, source2)
     recv_rows(rows2, SUB2)
 
     def prop2(d):
@@ -326,26 +391,22 @@
         lhs2[:, at] = jnp.concatenate([v, low], axis=0).astype(jnp.bfloat16)
 
     each(0, cells // block, split)
-    tall = min(256, points)
-
-    def gather_out(to, dst):
-        def tile(t):
-            base = to * points + t * tall
-            point = lax.broadcasted_iota(jnp.int32, (tall, cells), 0)
-            hot = jnp.where(point == slot[...] - base, 1.0, 0.0).astype(jnp.bfloat16)
-            r = lax.dot_general(
-                lhs2[...], hot, (((1,), (1,)), ((), ())), preferred_element_type=jnp.float32
-            )
-            dst[to, :, pl.ds(pl.multiple_of(t * tall, tall), tall)] = r[:pad] + r[pad:]
-
-        each(0, points // tall, tile)
-
-    def leave(o):
-        gather_out(lax.rem(me + o, n), sback)
-        out_copy(o).start()
-
-    each(1, n, leave)
-    gather_out(me, rback)
+    def gather_out(to, t, dst):
+        base = to * points + t * tall
+        point = lax.broadcasted_iota(jnp.int32, (tall, cells), 0)
+        hot = jnp.where(point == slot[...] - base, 1.0, 0.0).astype(jnp.bfloat16)
+        r = lax.dot_general(
+            lhs2[...], hot, (((1,), (1,)), ((), ())), preferred_element_type=jnp.float32
+        )
+        dst[to, :, pl.ds(pl.multiple_of(t * tall, tall), tall)] = r[:pad] + r[pad:]
+
+    def leave(i):
+        t, o = i // (n - 1), lax.rem(i, n - 1) + 1
+        gather_out(lax.rem(me + o, n), t, sback)
+        out_copy(o, t).start()
+
+    each(0, tiles * (n - 1), leave)
+    each(0, tiles, lambda t: gather_out(me, t, rback))
 
     def place(frm):
         for d in range(dirs):
@@ -356,7 +417,7 @@
     place(me)
 
     def back(o):
-        out_copy(o).wait_recv()
+        each(0, tiles, lambda t: out_copy(o, t).wait_recv())
         place(lax.rem(me + n - o, n))
 
     each(1, n, back)
@@ -366,18 +427,21 @@
 
     @pl.when(me < n - 1)
     def _():
-        to_upper.wait_send()
+        for c in to_upper:
+            c.wait_send()
 
     @pl.when(me > 0)
     def _():
-        to_lower.wait_send()
+        for c in to_lower:
+            c.wait_send()
 
     sent_rows(rows2, SUB2)
 
     def gone(o):
         par_copy(o).wait_send()
-        in_copy(o).wait_send()
-        out_copy(o).wait_send()
+        for part in range(len(cuts)):
+            in_copy(o, part).wait_send()
+        each(0, tiles, lambda t: out_copy(o, t).wait_send())
 
     each(1, n, gone)
 
@@ -385,10 +449,8 @@
 def shards(spectra, deal_slot, sea_mask, ice_class, brine, wind_rate, wind_dir, ice_table):
     dirs, freqs, _, points = spectra.shape
     n = lax.axis_size("cards")
-    me = lax.axis_index("cards")
     ns = lax.axis_size("sub")
     nrep = lax.axis_size("rep")
-    rep = lax.axis_index("rep")
     own = freqs // n
     rows, cols = sea_mask.shape
     cells = rows * cols
@@ -396,42 +458,27 @@
     comp = dirs * own
     pad = -(-comp // 8) * 8
 
-    theta = 2.0 * jnp.pi * jnp.arange(dirs * nrep, dtype=jnp.float32) / (dirs * nrep)
-    theta = lax.dynamic_slice_in_dim(theta, rep * dirs, dirs, 0)
-    ang = jnp.stack([jnp.cos(theta), jnp.sin(theta)])
-    freq = F0 * GROWTH ** jnp.arange(freqs, dtype=jnp.float32)
-    fall = jnp.concatenate(
-        [ice_table.T, (freq / freq[-1])[:, None], (COURANT * (freq[0] / freq))[:, None]], axis=1
-    )
-    fown = lax.dynamic_slice_in_dim(fall, me * own, own, 0)
-    wave = wind_rate[0]
-    point_rows = [
-        wave * jnp.cos(wind_dir[0]),
-        wave * jnp.sin(wind_dir[0]),
-        ice_class[0].astype(jnp.float32),
-        jnp.sqrt(brine[0] / 0.1),
-    ]
-    pts = jnp.stack(point_rows + [jnp.zeros_like(wave)] * 4)
-    col = lax.broadcasted_iota(jnp.int32, (rows, cols), 1).reshape(-1)
-    marks = jnp.stack(
-        [
-            sea_mask.reshape(-1).astype(jnp.float32),
-            (col != 0).astype(jnp.float32),
-            (col != cols - 1).astype(jnp.float32),
-        ]
-    )
+    theta = 2.0 * np.pi * np.arange(dirs * nrep) / (dirs * nrep)
+    ang = jnp.asarray(np.stack([np.cos(theta), np.sin(theta)]), jnp.float32)
+    freq = F0 * GROWTH ** np.arange(freqs)
+    shape = np.stack([freq / freq[-1], COURANT * (freq[0] / freq)], axis=1)
+    fall = jnp.concatenate([ice_table.T, jnp.asarray(shape, jnp.float32)], axis=1)
     f32 = jnp.float32
     vmem = pltpu.VMEM
-    count = 14 + 3 * n
-    sizes = (dirs, freqs, points, n, own, ns, nrep, classes, cols)
+    count = 20 + 3 * n + n * (points // min(256, points))
+    sizes = (dirs, freqs, points, n, own, ns, nrep, classes, rows, cols)
     spec = pl.BlockSpec(memory_space=pltpu.VMEM)
     result = pl.pallas_call(
         functools.partial(kernel, sizes),
         out_shape=jax.ShapeDtypeStruct((dirs, freqs, points), f32),
-        in_specs=[spec] * 4 + [pl.BlockSpec(memory_space=pltpu.SMEM)] + [spec] * 2,
+        in_specs=[spec] * 7 + [pl.BlockSpec(memory_space=pltpu.SMEM), spec],
         out_specs=spec,
         scratch_shapes=[
-            vmem((2, freqs, points), f32),
+            vmem((3, cells), f32),
+            vmem((8, points), f32),
+            pltpu.SMEM((2, dirs), f32),
+            vmem((own, classes + 2), f32),
+            vmem((2, freqs, 1, points), f32),
             vmem((n, pad, points), f32),
             vmem((n, pad, points), f32),
             vmem((n, 8, points), f32),
@@ -456,7 +503,7 @@
         compiler_params=pltpu.CompilerParams(
             collective_id=0, has_side_effects=True, vmem_limit_bytes=56 * 2**20
         ),
-    )(spectra.reshape(dirs, freqs, points), deal_slot, marks, pts, ang, fall, fown)
+    )(spectra, deal_slot, sea_mask, ice_class, brine, wind_rate, wind_dir, ang, fall)
     return result[:, :, None, :]
 
 

time: 166 us -> 150 us (0.904)
  the two profiles are of different devices: /device:TPU:11 before, /device:TPU:0 now
where the time goes in v3:
time: 150 us
  Pallas kernels  143 us (95%)
  local copies, waits for them, and re-layouts  6.29 us (4%)
    pallas_call x1, Pallas kernels, shards(): pl.pallas_call(functools.partial(kernel, sizes), out_shape=jax.ShapeDtype...  143 us
    broadcast_in_dim x1, local copies, waits for them, and re-layouts, shards(): return result[:, :, None, :]  5.6 us

profile of v3, /device:TPU:0, one launch (start us, length us, event | category | flops | bytes accessed | tf_op | source)
XLA Modules:
  0.0 149.8 jit_solution(5420400272987691352)
XLA Ops:
  0.0 0.7 pad_maximum_fusion
  0.7 0.7 copy.13.fall
  1.4 142.7 %shard_map.100 = f32[18,32,1024]{2,1,0:T(8,128)} custom-call(f32[18,32,1,1024]{3,2,1,0:T(1,128)} %x.1, s32[1,4096]{1,0:T(1,128)} %slot.1, s32[16,256]{1,0:T(8,128)} %sea.1, s32[1,1024]{1,0:T(1,128)} %ice_class.1, f32[1,1024]{1,0:T(1,128)} %brine.1, f32[1,1024]{1,0:T(1,128)} %wind_rate.1, f32[1,1024]{1,0:T(1,128)} %wind_dir.1, ...), custom_call_target="tpu_custom_call" | custom-call | tf_op jit(solution)/shard_map/pallas_call | solution.py:471
  144.2 5.6 %copy.14 = f32[18,32,1,1024]{3,2,1,0:T(1,128)} copy(f32[18,32,1,1024]{3,1,0,2:T(8,128)} %bitcast.2) | data formatting | bytes 4718592 | tf_op jit(solution)/shard_map/broadcast_in_dim | solution.py:507

commit v4 on v3

--- a/solution.py
+++ b/solution.py
@@ -157,26 +157,38 @@
     source1(dirs - 1, lambda at: halo[1, :, 0, at], lambda at: x[dirs - 2, :, 0, at])
     each(1, n, lambda o: in_copy(o, len(cuts) - 1).start())
 
-    half = pad + 8
     width = min(512, cells)
 
     count = cells // width
 
-    def gather_in(values, params, frm, first, between=None):
-        v = jnp.concatenate([values, params], axis=0)
+    def gather_in(frm, part, source, params, first, between=None):
+        low_row, high_row = cuts[part]
+        size = high_row - low_row
+        at_rows = pl.ds(low_row, size)
+        v = source[frm, at_rows, :]
+        if part == 0:
+            v = jnp.concatenate([v, params], axis=0)
+        m = v.shape[0]
         low = v - v.astype(jnp.bfloat16).astype(jnp.float32)
-        lhs[...] = jnp.concatenate([v, low], axis=0).astype(jnp.bfloat16)
+        two = lhs.at[pl.ds(0, 2 * m)]
+        two[...] = jnp.concatenate([v, low], axis=0).astype(jnp.bfloat16)
 
         def tile(t):
             at = pl.ds(pl.multiple_of(t * width, width), width)
             point = lax.broadcasted_iota(jnp.int32, (points, width), 0)
             hot = jnp.where(point == slot[:, at] - frm * points, 1.0, 0.0).astype(jnp.bfloat16)
-            r = jnp.dot(lhs[...], hot, preferred_element_type=jnp.float32)
-            r = r[:half] + r[half:]
+            r = jnp.dot(two[...], hot, preferred_element_type=jnp.float32)
+            r = r[:m] + r[m:]
             if first:
-                acc[:, at] = r
+                acc[at_rows, at] = r[:size]
             else:
-                acc[:, at] += r
+                acc[at_rows, at] += r[:size]
+            if part == 0:
+                extra = pl.ds(pad, 8)
+                if first:
+                    acc[extra, at] = r[size:]
+                else:
+                    acc[extra, at] += r[size:]
 
         tile(0)
         if count > 1:
@@ -184,8 +196,6 @@
         if between is not None:
             between()
         each(1, count - 1, tile)
-
-    gather_in(send[me], pts[...], me, True)
 
     def row_copies(rows, sem):
         last = pl.ds(cells - cols, cols)
@@ -253,15 +263,19 @@
         )
         return m * marks[0:1, :]
 
-    def arrived(o, between=None):
+    def arrived(o, part, between=None):
         frm = lax.rem(me + n - o, n)
-        par_copy(o).wait_recv()
-        for part in range(len(cuts)):
-            in_copy(o, part).wait_recv()
-        gather_in(recv[frm], precv[frm], frm, False, between)
-
-    each(1, n - 1, arrived)
-    arrived(n - 1, lambda: start_rows(rows1, SUB1))
+        if part == 0:
+            par_copy(o).wait_recv()
+        in_copy(o, part).wait_recv()
+        gather_in(frm, part, recv, precv[frm], False, between)
+
+    for part in range(len(cuts)):
+        gather_in(me, part, send, pts[...], True)
+        if part < len(cuts) - 1:
+            each(1, n, lambda o: arrived(o, part))
+    each(1, n - 1, lambda o: arrived(o, len(cuts) - 1))
+    arrived(n - 1, len(cuts) - 1, lambda: start_rows(rows1, SUB1))
 
     rate2[...] = rate_of(fown, acc[pad + 2 : pad + 3, :], acc[pad + 3 : pad + 4, :], classes)
     recv_rows(rows1, SUB1)

time: 150 us -> 148 us (0.987)
  Pallas kernels: 143 us -> 141 us
    pallas_call x1, Pallas kernels: 143 us -> 141 us  [shards(): pl.pallas_call(functools.partial(kernel, sizes), out_shape=jax.ShapeDtype...]
where the time goes in v4:
time: 148 us
  Pallas kernels  141 us (95%)
  local copies, waits for them, and re-layouts  6.29 us (4%)
    pallas_call x1, Pallas kernels, shards(): pl.pallas_call(functools.partial(kernel, sizes), out_shape=jax.ShapeDtype...  141 us
    broadcast_in_dim x1, local copies, waits for them, and re-layouts, shards(): return result[:, :, None, :]  5.6 us

profile of v4, /device:TPU:0, one launch (start us, length us, event | category | flops | bytes accessed | tf_op | source)
XLA Modules:
  0.0 147.5 jit_solution(18015617486791014475)
XLA Ops:
  0.0 0.7 pad_maximum_fusion
  0.7 0.7 copy.13.fall
  1.4 140.5 %shard_map.100 = f32[18,32,1024]{2,1,0:T(8,128)} custom-call(f32[18,32,1,1024]{3,2,1,0:T(1,128)} %x.1, s32[1,4096]{1,0:T(1,128)} %slot.1, s32[16,256]{1,0:T(8,128)} %sea.1, s32[1,1024]{1,0:T(1,128)} %ice_class.1, f32[1,1024]{1,0:T(1,128)} %brine.1, f32[1,1024]{1,0:T(1,128)} %wind_rate.1, f32[1,1024]{1,0:T(1,128)} %wind_dir.1, ...), custom_call_target="tpu_custom_call" | custom-call | tf_op jit(solution)/shard_map/pallas_call | solution.py:485
  141.9 5.6 %copy.14 = f32[18,32,1,1024]{3,2,1,0:T(1,128)} copy(f32[18,32,1,1024]{3,1,0,2:T(8,128)} %bitcast.2) | data formatting | bytes 4718592 | tf_op jit(solution)/shard_map/broadcast_in_dim | solution.py:521
